TPU v7x, 256 devices: a whole 4x4x8 slice. The times are simulated.
256 devices in a mesh: row: 8 (over z_hi, y), col: 32 (over z_lo, x, core).
Axes of the slice: x: 4, y: 4, z: 8 (z_hi: 2, z_lo: 4; z = z_hi * 4 + z_lo), core: 2. Of those that a mesh axis runs over, the one named last changes fastest.
Arguments:
- inputs: bfloat16 [1024, 12288], P('col', 'row'), may hold values from -6 to 6
- weight: bfloat16 [12288, 49152], P('row', 'col'), may hold values from -0.0546875 to 0.0546875
- hidden_bias: float32 [49152], P('col'), may hold values from -3 to 3
- act_cotangent: bfloat16 [1024, 49152], P('row', 'col'), may hold values from -6 to 6
Outputs:
- activated: bfloat16 [1024, 49152], P('row', 'col')
- input_grad: bfloat16 [1024, 12288], P('col', 'row')
- weight_grad: bfloat16 [12288, 49152], P('row', 'col')
- bias_grad: float32 [49152], P('col')
All inputs are finite; a program needn't handle non-finite values.
Results may differ from a plain program's by a relative error of at most 0.007.
Values may be sent and summed in bfloat16 or wider, within the bound.
A program may use at most 128 MiB of HBM per device.

v0:
```python
import math

import jax
import jax.numpy as jnp
from jax import lax
from jax.sharding import PartitionSpec as P

gelu_const = math.sqrt(2.0 / math.pi)


def gelu_value(value):
    inner = jnp.tanh(gelu_const * (value + 0.044715 * value * value * value))
    return 0.5 * value * (1.0 + inner)


def gelu_slope(value):
    inner = jnp.tanh(gelu_const * (value + 0.044715 * value * value * value))
    return 0.5 * (1.0 + inner) + 0.5 * value * (1.0 - inner * inner) * gelu_const * (
        1.0 + 3.0 * 0.044715 * value * value
    )


def local(inputs, weight, hidden_bias, act_cotangent):
    full_inputs = lax.all_gather(inputs, "col", axis=0, tiled=True)
    hidden = (
        lax.psum_scatter(
            jnp.dot(full_inputs, weight, preferred_element_type=jnp.float32),
            "row",
            scatter_dimension=0,
            tiled=True,
        )
        + hidden_bias[None, :]
    )
    activated = gelu_value(hidden).astype(jnp.bfloat16)
    hidden_cotangent = (act_cotangent.astype(jnp.float32) * gelu_slope(hidden)).astype(jnp.bfloat16)
    bias_grad = lax.psum(jnp.sum(hidden_cotangent.astype(jnp.float32), axis=0), "row")
    full_cotangent = lax.all_gather(hidden_cotangent, "row", axis=0, tiled=True)
    weight_grad = lax.dot_general(
        full_inputs, full_cotangent, (((0,), (0,)), ((), ())), preferred_element_type=jnp.float32
    ).astype(jnp.bfloat16)
    input_grad = lax.psum_scatter(
        lax.dot_general(
            full_cotangent, weight, (((1,), (1,)), ((), ())), preferred_element_type=jnp.float32
        ),
        "col",
        scatter_dimension=0,
        tiled=True,
    ).astype(jnp.bfloat16)
    return (activated, input_grad, weight_grad, bias_grad)


def solution(mesh):
    in_specs = (P("col", "row"), P("row", "col"), P("col"), P("row", "col"))
    out_specs = (P("row", "col"), P("col", "row"), P("row", "col"), P("col"))
    return jax.shard_map(local, mesh=mesh, in_specs=in_specs, out_specs=out_specs, check_vma=False)
```

profile of v0, /device:TPU:8, one launch (start us, length us, event | category | flops | bytes accessed | tf_op | source)
XLA Modules:
  0.0 496.3 jit_solution(4257729981342510045)
XLA Ops:
  7.2 0.0 all-gather.3.cloned.1.call-start
  7.2 0.7 all-gather.3.cloned.1.call-update
  7.9 0.0 reduce-scatter.3.cloned.1.call-start
  7.9 66.3 %all-gather.3.cloned.1.call-done = bf16[1024,1536]{1,0:T(8,128)(2,1)} async-done(((bf16[32,1536]{1,0:T(8,128)(2,1)}), bf16[1024,1536]{1,0:T(8,128)(2,1)}) %all-gather.3.cloned.1.call-update) | async-done | bytes 3145744 | tf_op jit(solution)/shard_map/all_gather | solution.py:24
  74.3 9.7 %fusion.9 = f32[1024,1536]{1,0:T(8,128)} fusion(bf16[1024,1536]{1,0:T(8,128)(2,1)} %all-gather.3.cloned.1.call-done, bf16[1536,1536]{1,0:T(8,128)(2,1)} %param.5), kind=kOutput, calls=%fused_computation.13 | convolution fusion | flops 4831838208 | bytes 14155776 | tf_op jit(solution)/shard_map/dot_general | solution.py:27
  84.0 0.0 copy-start
  84.0 0.0 copy-start.1
  84.0 0.0 reduce-scatter.3.cloned.1.call-update
  84.0 0.0 all-gather.5.cloned.1.call-start
  84.1 152.9 %reduce-scatter.3.cloned.1.call-done = f32[128,1536]{1,0:T(8,128)} async-done(((f32[1024,1536]{1,0:T(8,128)}), f32[128,1536]{1,0:T(8,128)}) %reduce-scatter.3.cloned.1.call-update) | async-done | bytes 786448 | tf_op jit(solution)/shard_map/reduce_scatter | solution.py:26
  237.0 0.0 copy-done
  237.0 0.0 copy-done.1
  237.0 2.6 convert_reduce_fusion
  239.6 0.0 all-gather.5.cloned.1.call-update
  239.7 0.0 reduce-scatter.5.cloned.1.call-start
  239.7 88.3 %all-gather.5.cloned.1.call-done = bf16[1024,1536]{1,0:T(8,128)(2,1)} async-done(((bf16[128,1536]{1,0:T(8,128)(2,1)}), bf16[1024,1536]{1,0:T(8,128)(2,1)}) %all-gather.5.cloned.1.call-update) | async-done | bytes 3145744 | tf_op jit(solution)/shard_map/all_gather | solution.py:37
  328.0 9.8 %fusion.10 = f32[1024,1536]{1,0:T(8,128)} fusion(bf16[1024,1536]{1,0:T(8,128)(2,1)} %all-gather.5.cloned.1.call-done, bf16[1536,1536]{1,0:T(8,128)(2,1)} %param.5), kind=kOutput, calls=%fused_computation.14 | convolution fusion | flops 4831838208 | bytes 14155776 | tf_op jit(solution)/shard_map/dot_general | solution.py:42
  337.8 0.0 reduce-scatter.5.cloned.1.call-update
  337.8 26.1 %psum.7 = f32[1536]{0:T(1024)} all-reduce(f32[1536]{0:T(1024)S(1)} %get-tuple-element.8), channel_id=1, replica_groups=mesh['row'=8,'col'=32] {'row'}, use_global_device_ids=true, to_apply=%region_3.0 | all-reduce | flops 1536 | bytes 12288 | tf_op jit(solution)/shard_map/psum | solution.py:36
  363.9 0.0 copy-done.2
  363.9 8.9 %fusion = bf16[1536,1536]{0,1:T(8,128)(2,1)} fusion(bf16[1024,1536]{1,0:T(8,128)(2,1)} %all-gather.5.cloned.1.call-done, bf16[1024,1536]{1,0:T(8,128)(2,1)S(1)} %copy-done.2), kind=kOutput, calls=%fused_computation.1 | convolution fusion | flops 4834197504 | bytes 11010048 | tf_op jit(solution)/shard_map/dot_general | solution.py:38
  372.8 6.6 %copy.8 = bf16[1536,1536]{1,0:T(8,128)(2,1)} copy(bf16[1536,1536]{0,1:T(8,128)(2,1)} %fusion) | data formatting | bytes 9437184
  379.4 108.8 %reduce-scatter.5.cloned.1.call-done = f32[32,1536]{1,0:T(8,128)} async-done(((f32[1024,1536]{1,0:T(8,128)}), f32[32,1536]{1,0:T(8,128)}) %reduce-scatter.5.cloned.1.call-update) | async-done | bytes 196624 | tf_op jit(solution)/shard_map/reduce_scatter | solution.py:41
  488.1 1.6 convert_element_type.24
  (1 shorter events, 0.0 us)
Async XLA Ops:
  7.2 67.1 %all-gather.3.cloned.1.call-start = ((), (), s32[]{:S(2)}) async-start(), calls=%async_computation.2 | async-start | bytes 3244032 | tf_op jit(solution)/shard_map/all_gather | solution.py:24
  7.9 229.1 %reduce-scatter.3.cloned.1.call-start = ((), (), s32[]{:S(2)}) async-start(), calls=%async_computation.3 | async-start | bytes 7077888 | tf_op jit(solution)/shard_map/reduce_scatter | solution.py:26
  84.0 153.0 %copy-start = (bf16[128,1536]{1,0:T(8,128)(2,1)S(1)}, bf16[128,1536]{1,0:T(8,128)(2,1)}, u32[]{:S(2)}) copy-start(bf16[128,1536]{1,0:T(8,128)(2,1)} %param.7) | copy-start | bytes 1179652
  84.0 153.0 %copy-start.1 = (f32[1536]{0:T(1024)S(1)}, f32[1536]{0:T(1024)}, u32[]{:S(2)}) copy-start(f32[1536]{0:T(1024)} %param.6) | copy-start | bytes 18436
  84.0 244.0 %all-gather.5.cloned.1.call-start = ((), (), s32[]{:S(2)}) async-start(), calls=%async_computation.4 | async-start | bytes 3538944 | tf_op jit(solution)/shard_map/all_gather | solution.py:37
  239.7 248.5 %reduce-scatter.5.cloned.1.call-start = ((), (), s32[]{:S(2)}) async-start(), calls=%async_computation.5 | async-start | bytes 6488064 | tf_op jit(solution)/shard_map/reduce_scatter | solution.py:41
  337.8 26.1 %copy-start.2 = (bf16[1024,1536]{1,0:T(8,128)(2,1)S(1)}, bf16[1024,1536]{1,0:T(8,128)(2,1)}, u32[]{:S(2)}) copy-start(bf16[1024,1536]{1,0:T(8,128)(2,1)} %all-gather.3.cloned.1.call-done) | copy-start | bytes 9437188
Sparse Core Ops, SparseCore 0:
  9.9 64.3 all-gather.2
  84.1 152.7 reduce-scatter.2
  240.5 87.4 all-gather.4
  337.9 150.1 reduce-scatter.4
where the time goes:
time: 497 us; the launch traced here: 496 us
  waiting for transfers between devices  417 us (84%)
  matrix products  28.3 us (6%)
  blocking collectives  26.1 us (5%)
  between operations  13.8 us (3%)
  local copies, waits for them, and re-layouts  6.63 us (1%)
    reduce_scatter x1, waiting for transfers between devices, local(): lax.psum_scatter(jnp.dot(full_inputs, weight, preferred_element_type=jnp....  153 us
    reduce_scatter x1, waiting for transfers between devices, local(): lax.psum_scatter(lax.dot_general(full_cotangent, weight, (((1,), (1,)), (...  109 us
    all_gather x1, waiting for transfers between devices, local(): full_cotangent = lax.all_gather(hidden_cotangent, 'row', axis=0, tiled=True)  88.3 us
    all_gather x1, waiting for transfers between devices, local(): full_inputs = lax.all_gather(inputs, 'col', axis=0, tiled=True)  66.3 us
    psum x1, blocking collectives, local(): lax.psum(jnp.sum(hidden_cotangent.astype(jnp.float32), axis=0), 'row')  26.1 us
  transfers between devices with their start and end apart: 4, of which 4 were waited for; matrix products, arithmetic and copies ran while one was open for 3% of the time, Pallas kernels for 0%

commit v1 on v0

v1 whole, which is shorter than its diff:
```python
import math

import jax
import jax.numpy as jnp
from jax import lax
from jax.experimental import pallas as pl
from jax.experimental.pallas import tpu as pltpu
from jax.sharding import PartitionSpec as P

gelu_const = math.sqrt(2.0 / math.pi)
BF = jnp.bfloat16
F32 = jnp.float32
MESH = pl.DeviceIdType.MESH

HALVES = 2
CH = 3
WIDTH = 1536
F = WIDTH // CH
UNITS = HALVES * CH


def dot_nn(a, b):
    return lax.dot_general(a, b, (((1,), (0,)), ((), ())), preferred_element_type=F32)


def dot_nt(a, b):
    return lax.dot_general(a, b, (((1,), (1,)), ((), ())), preferred_element_type=F32)


def dot_tn(a, b):
    return lax.dot_general(a, b, (((0,), (0,)), ((), ())), preferred_element_type=F32)


def kernel(
    x_hbm, w_hbm, bias_ref, ct_hbm,
    act_hbm, ig_ref, wg_hbm, bg_ref,
    X, W, CT, ACT, PH, RA, RB, RC, CB, ZS, ZR, OWN, COT,
    IGB, RK, S, XA, XB, XC, XM, T, ZT, WG,
    loc, wgsem, actsem,
    az, ax, af, ak, ry, rz, gz, gy, gf, ck, cx, cz,
    saz, sax, saf, sak, sry, srz, sgz, sgy, sgf, sck, scx, scz,
):
    r = lax.axis_index("row")
    c = lax.axis_index("col")
    zh, y = r // 4, r % 4
    zl, x, k = c // 8, (c // 2) % 4, c % 2

    yp = (zh * 4 + (y + 1) % 4, c)
    ym = (zh * 4 + (y + 3) % 4, c)
    zpart = ((1 - zh) * 4 + y, c)
    xp = (r, zl * 8 + ((x + 1) % 4) * 2 + k)
    xm = (r, zl * 8 + ((x + 3) % 4) * 2 + k)
    core = (r, zl * 8 + x * 2 + (1 - k))
    zls = [zl, zl + 1 - 2 * (zl % 2), (zl + 2) % 4, 3 - zl]
    zpeer = [None] + [(r, zls[m] * 8 + x * 2 + k) for m in (1, 2, 3)]
    xpeer = (xp, xm)

    started = []

    def remote(src, dst, ssem, rsem, dev):
        return pltpu.make_async_remote_copy(
            src_ref=src, dst_ref=dst, send_sem=ssem, recv_sem=rsem, device_id=dev, device_id_type=MESH
        )

    def send(*args):
        copy = remote(*args)
        copy.start()
        started.append(copy)

    def arrived(dst, rsem, ssem):
        remote(dst, dst, ssem, rsem, core).wait_recv()

    cp_x = [pltpu.make_async_copy(x_hbm.at[h], X.at[h, zl, x, k], loc.at[h]) for h in range(HALVES)]
    cp_w = pltpu.make_async_copy(w_hbm, W, loc.at[2])
    cp_ct = pltpu.make_async_copy(ct_hbm, CT, loc.at[3])
    for cp in cp_x:
        cp.start()
    cp_w.start()
    cp_ct.start()
    barrier = pltpu.get_barrier_semaphore()
    peers = [yp, ym, zpart, xp, xm, core] + zpeer[1:]
    for p in peers:
        pl.semaphore_signal(barrier, inc=1, device_id=p, device_id_type=MESH)
    pl.semaphore_wait(barrier, len(peers))
    for cp in cp_x:
        cp.wait()

    def ag_start(h):
        own = X.at[h, zl, x, k]
        for m in (1, 2, 3):
            send(own, own, saz.at[h, m - 1], az.at[h, m - 1], zpeer[m])
        for d in range(2):
            send(own, own, sax.at[h, d, 0], ax.at[h, d, 0], xpeer[d])

    def ag_z(h):
        for m in (1, 2, 3):
            blk = X.at[h, zls[m], x, k]
            arrived(blk, az.at[h, m - 1], saz.at[h, m - 1])
            for d in range(2):
                send(blk, blk, sax.at[h, d, m], ax.at[h, d, m], xpeer[d])
        col = X.at[h, :, x, k]
        send(col, col, sak.at[h, 0], ak.at[h, 0], core)

    def ag_f(h):
        for m in range(4):
            for d in range(2):
                blk = X.at[h, zls[m], (x + 3 - 2 * d) % 4, k]
                arrived(blk, ax.at[h, d, m], sax.at[h, d, m])
                if d == m // 2:
                    send(blk, blk, saf.at[h, m], af.at[h, m], xpeer[d])
        for d in range(2):
            col = X.at[h, :, (x + 3 - 2 * d) % 4, k]
            send(col, col, sak.at[h, 1 + d], ak.at[h, 1 + d], core)

    def ag_k(h):
        for m in range(4):
            blk = X.at[h, zls[m], (x + 2) % 4, k]
            arrived(blk, af.at[h, m], saf.at[h, m])
        col = X.at[h, :, (x + 2) % 4, k]
        send(col, col, sak.at[h, 3], ak.at[h, 3], core)

    def ag_done(h):
        for i, xx in enumerate((x, (x + 3) % 4, (x + 1) % 4, (x + 2) % 4)):
            col = X.at[h, :, xx, 1 - k]
            arrived(col, ak.at[h, i], sak.at[h, i])

    def cols(j):
        return pl.ds(j * F, F)

    def m1(u):
        h, j = divmod(u, CH)
        js = cols(j)
        part = dot_nn(X[h].reshape(512, WIDTH), W[:, js])
        PH[h, :, :, js] = part.astype(BF).reshape(8, 64, F)
        y1, y2, y3 = (y + 1) % 4, (y + 2) % 4, (y + 3) % 4
        send(PH.at[h, y2, :, js], RA.at[h, 0, :, js], sry.at[u, 0], ry.at[u, 0], yp)
        send(PH.at[h, y2 + 4, :, js], RA.at[h, 1, :, js], sry.at[u, 1], ry.at[u, 1], ym)
        send(PH.at[h, y1 + 4, :, js], RB.at[h, 1, :, js], sry.at[u, 2], ry.at[u, 2], yp)
        send(PH.at[h, y3, :, js], RB.at[h, 0, :, js], sry.at[u, 3], ry.at[u, 3], ym)

    def r1(u):
        h, j = divmod(u, CH)
        js = cols(j)
        for s in range(2):
            arrived(RA.at[h, s, :, js], ry.at[u, s], sry.at[u, s])
            nxt = (y + 1 + 2 * s) % 4 + 4 * s
            CB[h, s, :, js] = (PH[h, nxt, :, js].astype(F32) + RA[h, s, :, js].astype(F32)).astype(BF)
            send(CB.at[h, s, :, js], RC.at[h, s, :, js], sry.at[u, 4 + s], ry.at[u, 4 + s], (yp, ym)[s])

    def r2(u):
        h, j = divmod(u, CH)
        js = cols(j)
        for i, buf in ((2, RB.at[h, 1]), (3, RB.at[h, 0]), (4, RC.at[h, 0]), (5, RC.at[h, 1])):
            arrived(buf.at[:, js], ry.at[u, i], sry.at[u, i])

        def total(s):
            return (
                PH[h, y + 4 * s, :, js].astype(F32)
                + RB[h, s, :, js].astype(F32)
                + RC[h, s, :, js].astype(F32)
            )

        ZS[h, :, js] = total(1 - zh).astype(BF)
        send(ZS.at[h, :, js], ZR.at[h, :, js], srz.at[u], rz.at[u], zpart)
        OWN[h, :, js] = total(zh)

    def g(u):
        h, j = divmod(u, CH)
        js = cols(j)
        arrived(ZR.at[h, :, js], rz.at[u], srz.at[u])
        v = OWN[h, :, js] + ZR[h, :, js].astype(F32) + bias_ref[:, js]
        sq = v * v
        t = jnp.tanh(gelu_const * v * (1.0 + 0.044715 * sq))
        half = 0.5 * (1.0 + t)
        ACT[:, h, :, js] = (v * half).astype(BF).reshape(4, 16, F)
        slope = half + 0.5 * v * (1.0 - t * t) * gelu_const * (1.0 + 3.0 * 0.044715 * sq)
        ct = CT[:, h, :, js].reshape(64, F).astype(F32)
        COT[h, r, :, js] = (ct * slope).astype(BF)
        own = COT.at[h, r, :, js]
        send(own, own, sgz.at[u], gz.at[u], zpart)
        for d in range(2):
            send(own, own, sgy.at[u, d, zh], gy.at[u, d, zh], (yp, ym)[d])
        pltpu.make_async_copy(
            ACT.at[:, h, :, js], act_hbm.at[:, h, :, js], actsem.at[u]
        ).start()

    def yo(u):
        h, j = divmod(u, CH)
        js = cols(j)
        oth = COT.at[h, (1 - zh) * 4 + y, :, js]
        arrived(oth, gz.at[u], sgz.at[u])
        for d in range(2):
            send(oth, oth, sgy.at[u, d, 1 - zh], gy.at[u, d, 1 - zh], (yp, ym)[d])

    def fw(u, s):
        h, j = divmod(u, CH)
        js = cols(j)
        blk = COT.at[h, (y + 3 + 2 * s) % 4 + 4 * s, :, js]
        arrived(blk, gy.at[u, s, s], sgy.at[u, s, s])
        send(blk, blk, sgf.at[u, s], gf.at[u, s], (zh * 4 + (y + 1 + 2 * s) % 4, c))

    def fwo(u):
        fw(u, zh)

    def fwp(u):
        fw(u, 1 - zh)

    def gd(u):
        h, j = divmod(u, CH)
        js = cols(j)
        for s in range(2):
            d = 1 - s
            arrived(COT.at[h, (y + 3 - 2 * d) % 4 + 4 * s, :, js], gy.at[u, d, s], sgy.at[u, d, s])
            arrived(COT.at[h, (y + 2) % 4 + 4 * s, :, js], gf.at[u, s], sgf.at[u, s])

    def m3(h, n):
        ns = cols(n)
        part = dot_nt(COT[h].reshape(512, WIDTH), W[ns, :])
        IGB[h, :, :, :, :, ns] = part.astype(BF).reshape(4, 4, 2, 16, F)
        send(IGB.at[h, :, :, 1 - k, :, ns], RK.at[h, :, :, :, ns], sck.at[h, n], ck.at[h, n], core)

    def k1(h, n):
        ns = cols(n)
        arrived(RK.at[h, :, :, :, ns], ck.at[h, n], sck.at[h, n])
        S[h, :, :, :, ns] = (
            IGB[h, :, :, k, :, ns].astype(F32) + RK[h, :, :, :, ns].astype(F32)
        ).astype(BF)
        x1, x2, x3 = (x + 1) % 4, (x + 2) % 4, (x + 3) % 4
        lo, hi = pl.ds(0, 2), pl.ds(2, 2)
        send(S.at[h, lo, x2, :, ns], XA.at[h, 0, :, :, ns], scx.at[h, n, 0], cx.at[h, n, 0], xp)
        send(S.at[h, hi, x2, :, ns], XA.at[h, 1, :, :, ns], scx.at[h, n, 1], cx.at[h, n, 1], xm)
        send(S.at[h, hi, x1, :, ns], XB.at[h, 1, :, :, ns], scx.at[h, n, 2], cx.at[h, n, 2], xp)
        send(S.at[h, lo, x3, :, ns], XB.at[h, 0, :, :, ns], scx.at[h, n, 3], cx.at[h, n, 3], xm)

    def k2(h, n):
        ns = cols(n)
        for s in range(2):
            arrived(XA.at[h, s, :, :, ns], cx.at[h, n, s], scx.at[h, n, s])
            pair = pl.ds(2 * s, 2)
            XM[h, s, :, :, ns] = (
                S[h, pair, (x + 1 + 2 * s) % 4, :, ns].astype(F32) + XA[h, s, :, :, ns].astype(F32)
            ).astype(BF)
            send(
                XM.at[h, s, :, :, ns], XC.at[h, s, :, :, ns],
                scx.at[h, n, 4 + s], cx.at[h, n, 4 + s], xpeer[s],
            )

    def k3(h, n):
        ns = cols(n)
        for i, buf in ((2, XB.at[h, 1]), (3, XB.at[h, 0]), (4, XC.at[h, 0]), (5, XC.at[h, 1])):
            arrived(buf.at[:, :, ns], cx.at[h, n, i], scx.at[h, n, i])
        for s in range(2):
            pair = pl.ds(2 * s, 2)
            T[h, pair, :, ns] = (
                S[h, pair, x, :, ns].astype(F32)
                + XB[h, s, :, :, ns].astype(F32)
                + XC[h, s, :, :, ns].astype(F32)
            ).astype(BF)
        for m in (1, 2, 3):
            send(
                T.at[h, zls[m], :, ns], ZT.at[h, m - 1, :, ns],
                scz.at[h, n, m - 1], cz.at[h, n, m - 1], zpeer[m],
            )

    def k4(h, n):
        ns = cols(n)
        total = T[h, zl, :, ns].astype(F32)
        for m in (1, 2, 3):
            arrived(ZT.at[h, m - 1, :, ns], cz.at[h, n, m - 1], scz.at[h, n, m - 1])
            total = total + ZT[h, m - 1, :, ns].astype(F32)
        ig_ref[h, :, ns] = total.astype(BF)

    def m2(m, j):
        ms, js = cols(m), cols(j)
        a = X[:, :, :, :, :, ms].reshape(1024, F)
        b = COT[:, :, :, js].reshape(1024, F)
        WG[ms, js] = dot_tn(a, b).astype(BF)

    def m2_out(m):
        pltpu.make_async_copy(WG.at[cols(m)], wg_hbm.at[cols(m)], wgsem.at[m]).start()

    def bg(j):
        js = cols(j)
        bg_ref[:, js] = jnp.sum(COT[:, :, :, js].astype(F32).reshape(1024, F), axis=0, keepdims=True)

    ag_start(0)
    ag_z(0)
    ag_start(1)
    ag_f(0)
    ag_k(0)
    ag_done(0)
    cp_w.wait()
    cp_ct.wait()
    m1(0)
    ag_z(1)
    m1(1)
    r1(0)
    ag_f(1)
    m1(2)
    r1(1)
    r2(0)
    ag_k(1)
    r1(2)
    r2(1)
    ag_done(1)
    m1(3)
    r2(2)
    m1(4)
    r1(3)
    g(0)
    m1(5)
    r1(4)
    r2(3)
    g(1)
    yo(0)
    fwo(0)
    r1(5)
    r2(4)
    g(2)
    yo(1)
    fwo(1)
    fwp(0)
    r2(5)
    g(3)
    yo(2)
    fwo(2)
    fwp(1)
    g(4)
    yo(3)
    fwo(3)
    fwp(2)
    gd(0)
    gd(1)
    gd(2)
    for n in range(CH):
        m3(0, n)
    k1(0, 0)
    g(5)
    yo(4)
    fwo(4)
    fwp(3)
    k1(0, 1)
    k1(0, 2)
    k2(0, 0)
    yo(5)
    fwo(5)
    fwp(4)
    k2(0, 1)
    k2(0, 2)
    k3(0, 0)
    fwp(5)
    k3(0, 1)
    k3(0, 2)
    gd(3)
    gd(4)
    gd(5)
    m3(1, 0)
    m3(1, 1)
    k1(1, 0)
    m3(1, 2)
    k1(1, 1)
    k1(1, 2)
    for n in range(CH):
        k4(0, n)
    bg(0)
    k2(1, 0)
    bg(1)
    k2(1, 1)
    bg(2)
    k2(1, 2)
    m2(0, 0)
    m2(0, 1)
    k3(1, 0)
    m2(0, 2)
    m2_out(0)
    k3(1, 1)
    m2(1, 0)
    k3(1, 2)
    m2(1, 1)
    m2(1, 2)
    m2_out(1)
    m2(2, 0)
    m2(2, 1)
    m2(2, 2)
    m2_out(2)
    for n in range(CH):
        k4(1, n)

    for copy in started:
        copy.wait_send()
    for u in range(UNITS):
        h, j = divmod(u, CH)
        pltpu.make_async_copy(ACT.at[:, h, :, cols(j)], act_hbm.at[:, h, :, cols(j)], actsem.at[u]).wait()
    for m in range(CH):
        pltpu.make_async_copy(WG.at[cols(m)], wg_hbm.at[cols(m)], wgsem.at[m]).wait()


def local(inputs, weight, hidden_bias, act_cotangent):
    dma = pltpu.SemaphoreType.DMA
    sems = [
        (2, 3), (2, 2, 4), (2, 4), (2, 4),
        (UNITS, 6), (UNITS,), (UNITS,), (UNITS, 2, 2), (UNITS, 2),
        (2, CH), (2, CH, 6), (2, CH, 3),
    ]
    scratch = [
        pltpu.VMEM((2, 4, 4, 2, 16, WIDTH), BF),
        pltpu.VMEM((WIDTH, WIDTH), BF),
        pltpu.VMEM((4, 2, 16, WIDTH), BF),
        pltpu.VMEM((4, 2, 16, WIDTH), BF),
        pltpu.VMEM((2, 8, 64, WIDTH), BF),
        pltpu.VMEM((2, 2, 64, WIDTH), BF),
        pltpu.VMEM((2, 2, 64, WIDTH), BF),
        pltpu.VMEM((2, 2, 64, WIDTH), BF),
        pltpu.VMEM((2, 2, 64, WIDTH), BF),
        pltpu.VMEM((2, 64, WIDTH), BF),
        pltpu.VMEM((2, 64, WIDTH), BF),
        pltpu.VMEM((2, 64, WIDTH), F32),
        pltpu.VMEM((2, 8, 64, WIDTH), BF),
        pltpu.VMEM((2, 4, 4, 2, 16, WIDTH), BF),
        pltpu.VMEM((2, 4, 4, 16, WIDTH), BF),
        pltpu.VMEM((2, 4, 4, 16, WIDTH), BF),
        pltpu.VMEM((2, 2, 2, 16, WIDTH), BF),
        pltpu.VMEM((2, 2, 2, 16, WIDTH), BF),
        pltpu.VMEM((2, 2, 2, 16, WIDTH), BF),
        pltpu.VMEM((2, 2, 2, 16, WIDTH), BF),
        pltpu.VMEM((2, 4, 16, WIDTH), BF),
        pltpu.VMEM((2, 3, 16, WIDTH), BF),
        pltpu.VMEM((WIDTH, WIDTH), BF),
        dma((4,)), dma((CH,)), dma((UNITS,)),
    ] + [dma(s) for s in sems + sems]
    hbm = pl.BlockSpec(memory_space=pl.ANY)
    vmem = pl.BlockSpec(memory_space=pltpu.VMEM)
    act, ig, wg, bgr = pl.pallas_call(
        kernel,
        out_shape=(
            jax.ShapeDtypeStruct((4, 2, 16, WIDTH), BF),
            jax.ShapeDtypeStruct((2, 16, WIDTH), BF),
            jax.ShapeDtypeStruct((WIDTH, WIDTH), BF),
            jax.ShapeDtypeStruct((1, WIDTH), F32),
        ),
        in_specs=[hbm, hbm, vmem, hbm],
        out_specs=(hbm, vmem, hbm, vmem),
        scratch_shapes=scratch,
        compiler_params=pltpu.CompilerParams(
            collective_id=0, has_side_effects=True, vmem_limit_bytes=56 << 20
        ),
        name="ffn",
    )(
        inputs.reshape(2, 16, WIDTH),
        weight,
        hidden_bias.reshape(1, WIDTH),
        act_cotangent.reshape(4, 2, 16, WIDTH),
    )
    return act.reshape(128, WIDTH), ig.reshape(32, WIDTH), wg, bgr.reshape(WIDTH)


def solution(mesh):
    in_specs = (P("col", "row"), P("row", "col"), P("col"), P("row", "col"))
    out_specs = (P("row", "col"), P("col", "row"), P("row", "col"), P("col"))
    return jax.shard_map(local, mesh=mesh, in_specs=in_specs, out_specs=out_specs, check_vma=False)
```

time: 497 us -> 124 us (0.25)
  waiting for transfers between devices: 417 us -> 0 us
  Pallas kernels: 0 us -> 111 us
  matrix products: 28.3 us -> 0 us
  blocking collectives: 26.1 us -> 0 us
  between operations: 13.8 us -> 0.64 us
    reduce_scatter x2 -> x0, waiting for transfers between devices: 262 us -> none  [the longest x1 153 us: local(): lax.psum_scatter(jnp.dot(full_inputs, weight, preferred_element_type=jnp....]
    all_gather x2 -> x0, waiting for transfers between devices: 155 us -> none  [the longest x1 88.3 us: local(): full_cotangent = lax.all_gather(hidden_cotangent, 'row', axis=0, tiled=True)]
    pallas_call x0 -> x1, Pallas kernels: none -> 111 us  [local(): pl.pallas_call(kernel, out_shape=(jax.ShapeDtypeStruct((4, 2, 16, WIDTH),...]
    dot_general x3 -> x0, matrix products: 28.3 us -> none  [the longest x1 9.77 us: local(): lax.dot_general(full_cotangent, weight, (((1,), (1,)), ((), ())), preferr...]
    psum x1 -> x0, blocking collectives: 26.1 us -> none  [local(): lax.psum(jnp.sum(hidden_cotangent.astype(jnp.float32), axis=0), 'row')]
  transfers between devices with their start and end apart: 4 -> 0, of which waited for: 4 -> 0; matrix products, arithmetic and copies ran while one was open for 3% -> 0% of each run, Pallas kernels for 0% -> 0%
where the time goes in v1:
time: 124 us; the launch traced here: 123 us
  Pallas kernels  111 us (90%)
  local copies, waits for them, and re-layouts  9.42 us (8%)
  other arithmetic  1.31 us (1%)
    pallas_call x1, Pallas kernels, local(): pl.pallas_call(kernel, out_shape=(jax.ShapeDtypeStruct((4, 2, 16, WIDTH),...  111 us
    unnamed x3, local copies, waits for them, and re-layouts  8.13 us

profile of v1, /device:TPU:8, one launch (start us, length us, event | category | flops | bytes accessed | tf_op | source)
XLA Modules:
  0.0 122.7 jit_solution(9351550545917535228)
XLA Ops:
  0.6 1.3 %reshape.27.bias_ref = f32[1,1536]{1,0:T(1,128)} reshape(f32[1536]{0:T(1024)} %param.6) | data formatting | bytes 12288 | tf_op jit(solution)/shard_map/reshape | solution.py:451
  1.9 111.3 %ffn.1 = (bf16[4,2,16,1536]{3,2,1,0:T(8,128)(2,1)}, bf16[2,16,1536]{2,1,0:T(8,128)(2,1)}, bf16[1536,1536]{1,0:T(8,128)(2,1)}, f32[1,1536]{1,0:T(1,128)}) custom-call(bf16[2,16,1536]{2,1,0:T(8,128)(2,1)} %bitcast.7, bf16[1536,1536]{1,0:T(8,128)(2,1)} %w_hbm.1, f32[1,1536]{1,0:T(1,128)} %reshape.27.bias_ref, bf16[4,2,16,1536]{3,2,1,0:T(8,128)(2,1)} %bitcast.5), custom_call_target="tpu_custom_call" | custom-call | tf_op jit(solution)/shard_map/ffn/pallas_call | solution.py:433
  113.2 1.3 %reduce = f32[1536]{0:T(1024)} reduce(f32[1,1536]{1,0:T(1,128)} %get-tuple-element.11, f32[]{:T(128)} %constant), dimensions={0}, to_apply=%get-tuple-element.11.reduce_sub_computation | reduce | bytes 12292 | tf_op jit(solution)/shard_map/ffn/pallas_call | solution.py:433
  114.5 1.8 %copy.11 = bf16[128,1536]{1,0:T(8,128)(2,1)} copy(bf16[128,1536]{1,0:T(8,128)(2,1)} %bitcast.4) | data formatting | bytes 786432
  116.3 1.5 %copy.12 = bf16[32,1536]{1,0:T(8,128)(2,1)} copy(bf16[32,1536]{1,0:T(8,128)(2,1)} %bitcast.6) | data formatting | bytes 196608
  117.9 4.8 %copy.13 = bf16[1536,1536]{1,0:T(8,128)(2,1)} copy(bf16[1536,1536]{1,0:T(8,128)(2,1)} %get-tuple-element.18) | data formatting | bytes 9437184

commit v2 on v0

v2 whole, which is shorter than its diff:
```python
import math

import jax
import jax.numpy as jnp
from jax import lax
from jax.experimental import pallas as pl
from jax.experimental.pallas import tpu as pltpu
from jax.sharding import PartitionSpec as P

gelu_const = math.sqrt(2.0 / math.pi)
BF = jnp.bfloat16
F32 = jnp.float32
MESH = pl.DeviceIdType.MESH

WIDTH = 1536
Q = 4
J = 2
F = WIDTH // J
F2 = F // 2
UNITS = Q * J
NS = (1, 1, 2, 2)
NMAX = max(NS)


def dot_nn(a, b):
    return lax.dot_general(a, b, (((1,), (0,)), ((), ())), preferred_element_type=F32)


def dot_nt(a, b):
    return lax.dot_general(a, b, (((1,), (1,)), ((), ())), preferred_element_type=F32)


def dot_tn(a, b):
    return lax.dot_general(a, b, (((0,), (0,)), ((), ())), preferred_element_type=F32)


ORDER = (
    ("ag_start", 0), ("ag_start", 1), ("ag_z", 0), ("ag_z", 1), ("ag_f", 0), ("ag_z", 2), ("ag_f", 1),
    ("ag_k", 0), ("ag_z", 3), ("ag_done", 0), ("wload",), ("m1", 1), ("ag_k", 1), ("ag_f", 2),
    ("m1", 0), ("ag_done", 1), ("ag_f", 3), ("m1", 3), ("r1", 0), ("ag_k", 2), ("ag_k", 3),
    ("r1", 3), ("m1", 2), ("r1", 1), ("r2", 0), ("ag_done", 2), ("ag_done", 3), ("r2", 3),
    ("r1", 2), ("m1", 4), ("r2", 1), ("r2", 2), ("m1", 7), ("m1", 6), ("go", 0),
    ("m1", 5), ("go", 3), ("r1", 6), ("r1", 4), ("r1", 7), ("go", 2), ("go", 1),
    ("r2", 6), ("r1", 5), ("r2", 4), ("fo", 0), ("r2", 7), ("gn", 0), ("fo", 3),
    ("gn", 3), ("gn", 2), ("fn", 3), ("fo", 2), ("fo", 1), ("r2", 5), ("go", 4),
    ("fn", 2), ("gn", 1), ("gd", 3), ("go", 6), ("fn", 0), ("fn", 1), ("go", 5),
    ("gd", 2), ("go", 7), ("act_out",), ("gd", 0), ("m3", 1, 0), ("gd", 1), ("gn", 6),
    ("m3", 0, 0), ("fo", 5), ("fo", 6), ("k1", 1, 0), ("gn", 4), ("fo", 4), ("k1", 0, 0),
    ("gn", 7), ("k2", 1, 0), ("fo", 7), ("gn", 5), ("fn", 6), ("fn", 4), ("fn", 7),
    ("k2", 0, 0), ("k3", 1, 0), ("fn", 5), ("gd", 6), ("gd", 4), ("gd", 7), ("m3", 3, 1),
    ("m3", 3, 0), ("gd", 5), ("m3", 2, 1), ("k1", 3, 1), ("m3", 2, 0), ("k1", 3, 0), ("k1", 2, 1),
    ("m2", 1, 2), ("m2", 2, 2), ("k2", 3, 1), ("k1", 2, 0), ("k2", 3, 0), ("m2", 0, 2), ("m2", 1, 0),
    ("k2", 2, 1), ("k3", 0, 0), ("k2", 2, 0), ("k3", 3, 1), ("bg", 0), ("k3", 3, 0), ("k3", 2, 1),
    ("m2", 1, 1), ("m2_out", 1), ("bg", 1), ("k3", 2, 0), ("m2", 0, 1), ("m2", 0, 0), ("m2_out", 0),
    ("m2", 2, 0), ("m2", 2, 1), ("m2_out", 2), ("k4", 0), ("k4", 1),
)


def kernel(
    x_hbm, w_hbm, bias_ref, ct_hbm,
    act_hbm, ig_ref, wg_hbm, bg_ref,
    X, W, CT, ACT, PH, RA, RB, RC, CB, ZS, ZR, OWN, COT,
    IGB, RK, S, XA, XB, XC, XM, T, ZT, WG,
    loc, wgsem, actsem,
    az, ax, af, ak, ry, rz, gz, gy, gf, ck, cx, cz,
    saz, sax, saf, sak, sry, srz, sgz, sgy, sgf, sck, scx, scz,
):
    r = lax.axis_index("row")
    c = lax.axis_index("col")
    zh, y = r // 4, r % 4
    zl, x, k = c // 8, (c // 2) % 4, c % 2

    yp = (zh * 4 + (y + 1) % 4, c)
    ym = (zh * 4 + (y + 3) % 4, c)
    ypeer = (yp, ym)
    zpart = ((1 - zh) * 4 + y, c)
    xp = (r, zl * 8 + ((x + 1) % 4) * 2 + k)
    xm = (r, zl * 8 + ((x + 3) % 4) * 2 + k)
    xpeer = (xp, xm)
    core = (r, zl * 8 + x * 2 + (1 - k))
    zls = [zl, zl + 1 - 2 * (zl % 2), (zl + 2) % 4, 3 - zl]
    zpeer = [None] + [(r, zls[m] * 8 + x * 2 + k) for m in (1, 2, 3)]

    ss = [zl // 2, 1 - zl // 2] * 2
    owner = [zh == ss[q] for q in range(Q)]
    other = [zh != ss[q] for q in range(Q)]

    started = []

    def remote(src, dst, ssem, rsem, dev):
        return pltpu.make_async_remote_copy(
            src_ref=src, dst_ref=dst, send_sem=ssem, recv_sem=rsem, device_id=dev, device_id_type=MESH
        )

    def send(*args):
        copy = remote(*args)
        copy.start()
        started.append(copy)

    def arrived(dst, rsem, ssem):
        remote(dst, dst, ssem, rsem, core).wait_recv()

    cp_x = [pltpu.make_async_copy(x_hbm.at[h], X.at[h, zl, x, k], loc.at[h]) for h in range(2)]
    cp_w = pltpu.make_async_copy(w_hbm, W, loc.at[2])
    cp_ct = pltpu.make_async_copy(ct_hbm, CT, loc.at[3])
    for cp in cp_x:
        cp.start()
    cp_w.start()
    cp_ct.start()
    barrier = pltpu.get_barrier_semaphore()
    peers = [yp, ym, zpart, xp, xm, core] + zpeer[1:]
    for p in peers:
        pl.semaphore_signal(barrier, inc=1, device_id=p, device_id_type=MESH)
    pl.semaphore_wait(barrier, len(peers))
    for cp in cp_x:
        cp.wait()

    def wload():
        cp_w.wait()
        cp_ct.wait()

    def ag_start(h):
        own = X.at[h, zl, x, k]
        send(own, own, saz.at[h, 0], az.at[h, 0], zpeer[1])
        for d in range(2):
            send(own, own, sax.at[h, d, 0], ax.at[h, d, 0], xpeer[d])
        for m in (2, 3):
            send(own, own, saz.at[h, m - 1], az.at[h, m - 1], zpeer[m])

    def planes(q):
        return pl.ds(2 * ss[q], 2)

    def ag_z(q):
        h, p = divmod(q, 2)
        for m in ((1,), (2, 3))[p]:
            blk = X.at[h, zls[m], x, k]
            arrived(blk, az.at[h, m - 1], saz.at[h, m - 1])
            for d in range(2):
                send(blk, blk, sax.at[h, d, m], ax.at[h, d, m], xpeer[d])
        col = X.at[h, planes(q), x, k]
        send(col, col, sak.at[q, 0], ak.at[q, 0], core)

    def ag_f(q):
        h, p = divmod(q, 2)
        for m in (2 * p, 2 * p + 1):
            for d in (m % 2, 1 - m % 2):
                blk = X.at[h, zls[m], (x + 3 - 2 * d) % 4, k]
                arrived(blk, ax.at[h, d, m], sax.at[h, d, m])
                if d == m % 2:
                    send(blk, blk, saf.at[h, m], af.at[h, m], xpeer[d])
        for d in range(2):
            col = X.at[h, planes(q), (x + 3 - 2 * d) % 4, k]
            send(col, col, sak.at[q, 1 + d], ak.at[q, 1 + d], core)

    def ag_k(q):
        h, p = divmod(q, 2)
        for m in (2 * p, 2 * p + 1):
            blk = X.at[h, zls[m], (x + 2) % 4, k]
            arrived(blk, af.at[h, m], saf.at[h, m])
        col = X.at[h, planes(q), (x + 2) % 4, k]
        send(col, col, sak.at[q, 3], ak.at[q, 3], core)

    def ag_done(q):
        for i, xx in enumerate((x, (x + 3) % 4, (x + 1) % 4, (x + 2) % 4)):
            col = X.at[q // 2, planes(q), xx, 1 - k]
            arrived(col, ak.at[q, i], sak.at[q, i])

    def cols(j):
        return pl.ds(j * F, F)

    def side(j, a):
        return pl.ds(j * F + a * F2, F2)

    def m1(u):
        q, j = divmod(u, J)
        part = dot_nn(X[q // 2, planes(q)].reshape(256, WIDTH), W[:, cols(j)])
        PH[q, :, :, cols(j)] = part.astype(BF).reshape(4, 64, F)
        for i, d, near, a in ((0, 0, 2, 0), (1, 1, 2, 1), (2, 0, 1, 1), (3, 1, 3, 0)):
            buf = RA if i < 2 else RB
            send(
                PH.at[q, (y + near) % 4, :, side(j, a)], buf.at[q, :, side(j, a)],
                sry.at[u, i], ry.at[u, i], ypeer[d],
            )

    def r1(u):
        q, j = divmod(u, J)
        for a in range(2):
            sl = side(j, a)
            arrived(RA.at[q, :, sl], ry.at[u, a], sry.at[u, a])
            CB[q, :, sl] = (
                PH[q, (y + 1 + 2 * a) % 4, :, sl].astype(F32) + RA[q, :, sl].astype(F32)
            ).astype(BF)
            send(CB.at[q, :, sl], RC.at[q, :, sl], sry.at[u, 4 + a], ry.at[u, 4 + a], ypeer[a])

    def r2(u):
        q, j = divmod(u, J)
        js = cols(j)
        for i, buf, a in ((2, RB, 1), (3, RB, 0), (4, RC, 0), (5, RC, 1)):
            arrived(buf.at[q, :, side(j, a)], ry.at[u, i], sry.at[u, i])
        total = PH[q, y, :, js].astype(F32) + RB[q, :, js].astype(F32) + RC[q, :, js].astype(F32)

        @pl.when(owner[q])
        def _():
            OWN[q, :, js] = total

        @pl.when(other[q])
        def _():
            ZS[q, :, js] = total.astype(BF)
            remote(ZS.at[q, :, js], ZR.at[q, :, js], srz.at[u], rz.at[u], zpart).start()

    def share(u, yy):
        q, j = divmod(u, J)
        return COT.at[q // 2, ss[q] * 4 + yy, :, cols(j)]

    def give(u):
        for d in range(2):
            blk = share(u, y)
            remote(blk, blk, sgy.at[u, d], gy.at[u, d], ypeer[d]).start()

    def go(u):
        q, j = divmod(u, J)
        h, js = q // 2, cols(j)

        @pl.when(owner[q])
        def _():
            arrived(ZR.at[q, :, js], rz.at[u], srz.at[u])
            bias = jnp.concatenate(
                [bias_ref[pl.ds(j * (F // 128) + i, 1), :] for i in range(F // 128)], axis=1
            )
            v = OWN[q, :, js] + ZR[q, :, js].astype(F32) + bias
            sq = v * v
            t = jnp.tanh(gelu_const * v * (1.0 + 0.044715 * sq))
            half = 0.5 * (1.0 + t)
            slope = half + 0.5 * v * (1.0 - t * t) * gelu_const * (1.0 + 3.0 * 0.044715 * sq)
            ct = CT[:, h, :, js].reshape(64, F).astype(F32)
            COT[h, r, :, js] = (ct * slope).astype(BF)
            blk = share(u, y)
            remote(blk, blk, sgz.at[u], gz.at[u], zpart).start()
            give(u)
            ACT[:, h, :, js] = (v * half).astype(BF).reshape(4, 16, F)

    def gn(u):
        @pl.when(other[u // J])
        def _():
            arrived(share(u, y), gz.at[u], sgz.at[u])
            give(u)

    def fw(u):
        q, j = divmod(u, J)
        for d in range(2):
            yy = (y + 3 - 2 * d) % 4
            arrived(share(u, yy), gy.at[u, d], sgy.at[u, d])
            blk = COT.at[q // 2, ss[q] * 4 + yy, :, side(j, d)]
            remote(blk, blk, sgf.at[u, d], gf.at[u, d], ypeer[d]).start()

    def fo(u):
        @pl.when(owner[u // J])
        def _():
            fw(u)

    def fn(u):
        @pl.when(other[u // J])
        def _():
            fw(u)

    def gd(u):
        q, j = divmod(u, J)
        for d in range(2):
            blk = COT.at[q // 2, ss[q] * 4 + (y + 2) % 4, :, side(j, d)]
            arrived(blk, gf.at[u, d], sgf.at[u, d])

    def feats(q, n):
        w = WIDTH // NS[q]
        return pl.ds(n * w, w)

    def m3(q, n):
        w = WIDTH // NS[q]
        step = 512 if w % 512 == 0 else w
        cot = COT[q // 2, pl.ds(4 * ss[q], 4)].reshape(256, WIDTH)
        for i in range(w // step):
            sl = pl.ds(n * w + i * step, step)
            IGB[q, :, :, :, :, sl] = dot_nt(cot, W[sl, :]).astype(BF).reshape(2, 4, 2, 16, step)
        ns = feats(q, n)
        send(IGB.at[q, :, :, 1 - k, :, ns], RK.at[q, :, :, :, ns], sck.at[q, n], ck.at[q, n], core)

    def k1(q, n):
        ns = feats(q, n)
        arrived(RK.at[q, :, :, :, ns], ck.at[q, n], sck.at[q, n])
        S[q, :, :, :, ns] = (
            IGB[q, :, :, k, :, ns].astype(F32) + RK[q, :, :, :, ns].astype(F32)
        ).astype(BF)
        for i, d, near, a in ((0, 0, 2, 0), (1, 1, 2, 1), (2, 0, 1, 1), (3, 1, 3, 0)):
            buf = XA if i < 2 else XB
            send(
                S.at[q, a, (x + near) % 4, :, ns], buf.at[q, a, :, ns],
                scx.at[q, n, i], cx.at[q, n, i], xpeer[d],
            )

    def k2(q, n):
        ns = feats(q, n)
        for a in range(2):
            arrived(XA.at[q, a, :, ns], cx.at[q, n, a], scx.at[q, n, a])
            XM[q, a, :, ns] = (
                S[q, a, (x + 1 + 2 * a) % 4, :, ns].astype(F32) + XA[q, a, :, ns].astype(F32)
            ).astype(BF)
            send(XM.at[q, a, :, ns], XC.at[q, a, :, ns], scx.at[q, n, 4 + a], cx.at[q, n, 4 + a], xpeer[a])

    def k3(q, n):
        h, p = divmod(q, 2)
        ns = feats(q, n)
        for i, buf, a in ((2, XB, 1), (3, XB, 0), (4, XC, 0), (5, XC, 1)):
            arrived(buf.at[q, a, :, ns], cx.at[q, n, i], scx.at[q, n, i])
        T[q, :, :, ns] = (
            S[q, :, x, :, ns].astype(F32) + XB[q, :, :, ns].astype(F32) + XC[q, :, :, ns].astype(F32)
        ).astype(BF)
        for m in ((1,), (2, 3))[p]:
            send(
                T.at[q, zls[m] % 2, :, ns], ZT.at[h, m - 1, :, ns],
                scz.at[h, m - 1, n], cz.at[h, m - 1, n], zpeer[m],
            )

    def k4(h):
        for m in (1, 2, 3):
            q = 2 * h + (m > 1)
            for n in range(NS[q]):
                ns = feats(q, n)
                arrived(ZT.at[h, m - 1, :, ns], cz.at[h, m - 1, n], scz.at[h, m - 1, n])
        total = T[2 * h, zl % 2].astype(F32)
        for m in (1, 2, 3):
            total = total + ZT[h, m - 1].astype(F32)
        ig_ref[h] = total.astype(BF)

    def third(m):
        return pl.ds(m * 512, 512)

    def m2(m, j):
        a = X[:, :, :, :, :, third(m)].reshape(1024, 512)
        b = COT[:, :, :, third(j)].reshape(1024, 512)
        WG[third(m), third(j)] = dot_tn(a, b).astype(BF)

    def wg_copy(m):
        return pltpu.make_async_copy(WG.at[third(m)], wg_hbm.at[third(m)], wgsem.at[m])

    def m2_out(m):
        wg_copy(m).start()

    def act_copy():
        return pltpu.make_async_copy(ACT, act_hbm, actsem.at[0])

    def act_out():
        act_copy().start()

    def bg(j):
        w = WIDTH // 2
        total = jnp.sum(COT[:, :, :, pl.ds(j * w, w)].astype(F32).reshape(1024, w), axis=0, keepdims=True)
        for i in range(w // 128):
            bg_ref[pl.ds(j * (w // 128) + i, 1), :] = total[:, i * 128 : (i + 1) * 128]

    stages = dict(
        ag_start=ag_start, ag_z=ag_z, ag_f=ag_f, ag_k=ag_k, ag_done=ag_done, wload=wload,
        m1=m1, r1=r1, r2=r2, go=go, gn=gn, fo=fo, fn=fn, gd=gd,
        m3=m3, k1=k1, k2=k2, k3=k3, k4=k4, m2=m2, m2_out=m2_out, bg=bg, act_out=act_out,
    )
    for name, *args in ORDER:
        stages[name](*args)

    for copy in started:
        copy.wait_send()
    for u in range(UNITS):
        q, j = divmod(u, J)
        js = cols(j)

        @pl.when(other[q])
        def _():
            remote(ZS.at[q, :, js], ZR.at[q, :, js], srz.at[u], rz.at[u], zpart).wait_send()

        @pl.when(owner[q])
        def _():
            remote(share(u, y), share(u, y), sgz.at[u], gz.at[u], zpart).wait_send()

        for d in range(2):
            remote(share(u, y), share(u, y), sgy.at[u, d], gy.at[u, d], ypeer[d]).wait_send()
            blk = COT.at[q // 2, ss[q] * 4 + (y + 3 - 2 * d) % 4, :, side(j, d)]
            remote(blk, blk, sgf.at[u, d], gf.at[u, d], ypeer[d]).wait_send()
    act_copy().wait()
    for m in range(3):
        wg_copy(m).wait()


def hand_out(*refs):
    srcs, dsts, bufs, sems = refs[:4], refs[4:8], refs[8:12], refs[12]
    pieces = []
    for src, buf, dst in zip(srcs, bufs, dsts):
        parts = 8 if src.shape[0] == WIDTH else 1
        rows = src.shape[0] // parts
        pieces += [tuple(v.at[pl.ds(p * rows, rows)] for v in (src, buf, dst)) for p in range(parts)]
    ins = [pltpu.make_async_copy(s, b, sems.at[0, i]) for i, (s, b, _) in enumerate(pieces)]
    outs = [pltpu.make_async_copy(b, d, sems.at[1, i]) for i, (_, b, d) in enumerate(pieces)]
    for cp in ins:
        cp.start()
    for i, o in zip(ins, outs):
        i.wait()
        o.start()
    for o in outs:
        o.wait()


def local(inputs, weight, hidden_bias, act_cotangent):
    dma = pltpu.SemaphoreType.DMA
    sems = [
        (2, 3), (2, 2, 4), (2, 4), (Q, 4),
        (UNITS, 6), (UNITS,), (UNITS,), (UNITS, 2), (UNITS, 2),
        (Q, NMAX), (Q, NMAX, 6), (2, 3, NMAX),
    ]
    scratch = [
        pltpu.VMEM((2, 4, 4, 2, 16, WIDTH), BF),
        pltpu.VMEM((WIDTH, WIDTH), BF),
        pltpu.VMEM((4, 2, 16, WIDTH), BF),
        pltpu.VMEM((4, 2, 16, WIDTH), BF),
        pltpu.VMEM((Q, 4, 64, WIDTH), BF),
        pltpu.VMEM((Q, 64, WIDTH), BF),
        pltpu.VMEM((Q, 64, WIDTH), BF),
        pltpu.VMEM((Q, 64, WIDTH), BF),
        pltpu.VMEM((Q, 64, WIDTH), BF),
        pltpu.VMEM((Q, 64, WIDTH), BF),
        pltpu.VMEM((Q, 64, WIDTH), BF),
        pltpu.VMEM((Q, 64, WIDTH), F32),
        pltpu.VMEM((2, 8, 64, WIDTH), BF),
        pltpu.VMEM((Q, 2, 4, 2, 16, WIDTH), BF),
        pltpu.VMEM((Q, 2, 4, 16, WIDTH), BF),
        pltpu.VMEM((Q, 2, 4, 16, WIDTH), BF),
        pltpu.VMEM((Q, 2, 16, WIDTH), BF),
        pltpu.VMEM((Q, 2, 16, WIDTH), BF),
        pltpu.VMEM((Q, 2, 16, WIDTH), BF),
        pltpu.VMEM((Q, 2, 16, WIDTH), BF),
        pltpu.VMEM((Q, 2, 16, WIDTH), BF),
        pltpu.VMEM((2, 3, 16, WIDTH), BF),
        pltpu.VMEM((WIDTH, WIDTH), BF),
        dma((4,)), dma((3,)), dma((1,)),
    ] + [dma(s) for s in sems + sems]
    hbm = pl.BlockSpec(memory_space=pl.ANY)
    vmem = pl.BlockSpec(memory_space=pltpu.VMEM)
    shapes = (
        jax.ShapeDtypeStruct((4, 2, 16, WIDTH), BF),
        jax.ShapeDtypeStruct((2, 16, WIDTH), BF),
        jax.ShapeDtypeStruct((WIDTH, WIDTH), BF),
        jax.ShapeDtypeStruct((WIDTH // 128, 128), F32),
    )
    results = pl.pallas_call(
        kernel,
        out_shape=shapes,
        in_specs=[hbm, hbm, vmem, hbm],
        out_specs=(hbm, vmem, hbm, vmem),
        scratch_shapes=scratch,
        compiler_params=pltpu.CompilerParams(
            collective_id=0, has_side_effects=True, vmem_limit_bytes=56 << 20
        ),
        name="ffn",
    )(
        inputs.reshape(2, 16, WIDTH),
        weight,
        hidden_bias.reshape(WIDTH // 128, 128),
        act_cotangent.reshape(4, 2, 16, WIDTH),
    )
    act, ig, wg, bgr = pl.pallas_call(
        hand_out,
        out_shape=shapes,
        in_specs=[hbm] * 4,
        out_specs=(hbm,) * 4,
        scratch_shapes=[pltpu.VMEM(v.shape, v.dtype) for v in shapes] + [dma((2, 11))],
        compiler_params=pltpu.CompilerParams(vmem_limit_bytes=56 << 20),
        name="hand_out",
    )(*results)
    return act.reshape(128, WIDTH), ig.reshape(32, WIDTH), wg, bgr.reshape(WIDTH)


def solution(mesh):
    in_specs = (P("col", "row"), P("row", "col"), P("col"), P("row", "col"))
    out_specs = (P("row", "col"), P("col", "row"), P("row", "col"), P("col"))
    return jax.shard_map(local, mesh=mesh, in_specs=in_specs, out_specs=out_specs, check_vma=False)
```

time: 497 us -> 110 us (0.22)
  waiting for transfers between devices: 417 us -> 0 us
  Pallas kernels: 0 us -> 109 us
  matrix products: 28.3 us -> 0 us
  blocking collectives: 26.1 us -> 0 us
  between operations: 13.8 us -> 0.8 us
  local copies, waits for them, and re-layouts: 6.63 us -> 0 us
    reduce_scatter x2 -> x0, waiting for transfers between devices: 262 us -> none  [the longest x1 153 us: local(): lax.psum_scatter(jnp.dot(full_inputs, weight, preferred_element_type=jnp....]
    all_gather x2 -> x0, waiting for transfers between devices: 155 us -> none  [the longest x1 88.3 us: local(): full_cotangent = lax.all_gather(hidden_cotangent, 'row', axis=0, tiled=True)]
    pallas_call x0 -> x2, Pallas kernels: none -> 109 us  [the longest x1 104 us: local(): pl.pallas_call(kernel, out_shape=shapes, in_specs=[hbm, hbm, vmem, hbm],...]
    dot_general x3 -> x0, matrix products: 28.3 us -> none  [the longest x1 9.77 us: local(): lax.dot_general(full_cotangent, weight, (((1,), (1,)), ((), ())), preferr...]
    psum x1 -> x0, blocking collectives: 26.1 us -> none  [local(): lax.psum(jnp.sum(hidden_cotangent.astype(jnp.float32), axis=0), 'row')]
    unnamed x7 -> x0, local copies, waits for them, and re-layouts: 6.63 us -> none
  transfers between devices with their start and end apart: 4 -> 0, of which waited for: 4 -> 0; matrix products, arithmetic and copies ran while one was open for 3% -> 0% of each run, Pallas kernels for 0% -> 0%
where the time goes in v2:
time: 110 us
  Pallas kernels  109 us (99%)
    pallas_call x1, Pallas kernels, local(): pl.pallas_call(kernel, out_shape=shapes, in_specs=[hbm, hbm, vmem, hbm],...  104 us
    pallas_call x1, Pallas kernels, local(): pl.pallas_call(hand_out, out_shape=shapes, in_specs=[hbm] * 4, out_specs=...  4.93 us

profile of v2, /device:TPU:8, one launch (start us, length us, event | category | flops | bytes accessed | tf_op | source)
XLA Modules:
  0.0 109.9 jit_solution(15207714576166732666)
XLA Ops:
  0.6 104.2 %ffn.1 = (bf16[4,2,16,1536]{3,2,1,0:T(8,128)(2,1)}, bf16[2,16,1536]{2,1,0:T(8,128)(2,1)}, bf16[1536,1536]{1,0:T(8,128)(2,1)}, f32[12,128]{1,0:T(8,128)}) custom-call(bf16[2,16,1536]{2,1,0:T(8,128)(2,1)} %bitcast.7, bf16[1536,1536]{1,0:T(8,128)(2,1)} %w_hbm.1, f32[12,128]{1,0:T(8,128)} %bitcast.8, bf16[4,2,16,1536]{3,2,1,0:T(8,128)(2,1)} %bitcast.6), custom_call_target="tpu_custom_call" | custom-call | tf_op jit(solution)/shard_map/ffn/pallas_call | solution.py:449
  104.9 4.9 %hand_out.1 = (bf16[4,2,16,1536]{3,2,1,0:T(8,128)(2,1)}, bf16[2,16,1536]{2,1,0:T(8,128)(2,1)}, bf16[1536,1536]{1,0:T(8,128)(2,1)}, f32[12,128]{1,0:T(8,128)}) custom-call(bf16[4,2,16,1536]{3,2,1,0:T(8,128)(2,1)} %get-tuple-element.12.refs_0_, bf16[2,16,1536]{2,1,0:T(8,128)(2,1)} %get-tuple-element.13.refs_1_, bf16[1536,1536]{1,0:T(8,128)(2,1)} %get-tuple-element.14.refs_2_, ...), custom_call_target="tpu_custom_call" | custom-call | tf_op jit(solution)/shard_map/hand_out/pallas_call | solution.py:465

commit v3 on v2

--- a/solution.py
+++ b/solution.py
@@ -18,7 +18,7 @@
 F = WIDTH // J
 F2 = F // 2
 UNITS = Q * J
-NS = (1, 1, 2, 2)
+NS = (1, 1, 1, 2)
 NMAX = max(NS)
 
 
@@ -36,23 +36,23 @@
 
 ORDER = (
     ("ag_start", 0), ("ag_start", 1), ("ag_z", 0), ("ag_z", 1), ("ag_f", 0), ("ag_z", 2), ("ag_f", 1),
-    ("ag_k", 0), ("ag_z", 3), ("ag_done", 0), ("wload",), ("m1", 1), ("ag_k", 1), ("ag_f", 2),
-    ("m1", 0), ("ag_done", 1), ("ag_f", 3), ("m1", 3), ("r1", 0), ("ag_k", 2), ("ag_k", 3),
-    ("r1", 3), ("m1", 2), ("r1", 1), ("r2", 0), ("ag_done", 2), ("ag_done", 3), ("r2", 3),
-    ("r1", 2), ("m1", 4), ("r2", 1), ("r2", 2), ("m1", 7), ("m1", 6), ("go", 0),
-    ("m1", 5), ("go", 3), ("r1", 6), ("r1", 4), ("r1", 7), ("go", 2), ("go", 1),
-    ("r2", 6), ("r1", 5), ("r2", 4), ("fo", 0), ("r2", 7), ("gn", 0), ("fo", 3),
-    ("gn", 3), ("gn", 2), ("fn", 3), ("fo", 2), ("fo", 1), ("r2", 5), ("go", 4),
-    ("fn", 2), ("gn", 1), ("gd", 3), ("go", 6), ("fn", 0), ("fn", 1), ("go", 5),
-    ("gd", 2), ("go", 7), ("act_out",), ("gd", 0), ("m3", 1, 0), ("gd", 1), ("gn", 6),
-    ("m3", 0, 0), ("fo", 5), ("fo", 6), ("k1", 1, 0), ("gn", 4), ("fo", 4), ("k1", 0, 0),
-    ("gn", 7), ("k2", 1, 0), ("fo", 7), ("gn", 5), ("fn", 6), ("fn", 4), ("fn", 7),
-    ("k2", 0, 0), ("k3", 1, 0), ("fn", 5), ("gd", 6), ("gd", 4), ("gd", 7), ("m3", 3, 1),
-    ("m3", 3, 0), ("gd", 5), ("m3", 2, 1), ("k1", 3, 1), ("m3", 2, 0), ("k1", 3, 0), ("k1", 2, 1),
-    ("m2", 1, 2), ("m2", 2, 2), ("k2", 3, 1), ("k1", 2, 0), ("k2", 3, 0), ("m2", 0, 2), ("m2", 1, 0),
-    ("k2", 2, 1), ("k3", 0, 0), ("k2", 2, 0), ("k3", 3, 1), ("bg", 0), ("k3", 3, 0), ("k3", 2, 1),
-    ("m2", 1, 1), ("m2_out", 1), ("bg", 1), ("k3", 2, 0), ("m2", 0, 1), ("m2", 0, 0), ("m2_out", 0),
-    ("m2", 2, 0), ("m2", 2, 1), ("m2_out", 2), ("k4", 0), ("k4", 1),
+    ("ag_k", 0), ("ag_z", 3), ("ag_done", 0), ("wload",), ("m1", 0), ("ag_k", 1), ("m1", 1),
+    ("ag_done", 1), ("m1", 3), ("ag_f", 3), ("ag_f", 2), ("r1", 1), ("r1", 3), ("m1", 2),
+    ("ag_k", 2), ("ag_k", 3), ("r2", 1), ("r1", 0), ("r2", 3), ("ag_done", 2), ("r1", 2),
+    ("m1", 5), ("r2", 0), ("m1", 4), ("r2", 2), ("ag_done", 3), ("m1", 6), ("r1", 5),
+    ("r1", 4), ("go", 3), ("go", 1), ("r1", 6), ("m1", 7), ("r2", 5), ("go", 0),
+    ("r2", 4), ("r2", 6), ("r1", 7), ("fo", 0), ("go", 2), ("gn", 1), ("fo", 3),
+    ("fo", 1), ("gn", 0), ("fn", 1), ("r2", 7), ("go", 6), ("fn", 0), ("gn", 3),
+    ("go", 5), ("go", 7), ("go", 4), ("act_out",), ("gd", 0), ("gn", 2), ("fo", 6),
+    ("gd", 1), ("gn", 5), ("fn", 3), ("m3", 0, 0), ("fo", 2), ("fn", 2), ("fo", 4),
+    ("gd", 3), ("gn", 4), ("gn", 6), ("fn", 5), ("fo", 5), ("gd", 2), ("k1", 0, 0),
+    ("gn", 7), ("m3", 1, 0), ("fn", 4), ("fn", 6), ("k2", 0, 0), ("k1", 1, 0), ("fn", 7),
+    ("fo", 7), ("gd", 5), ("gd", 4), ("m3", 2, 0), ("gd", 6), ("k2", 1, 0), ("gd", 7),
+    ("m3", 3, 0), ("k1", 2, 0), ("m3", 3, 1), ("k3", 0, 0), ("k1", 3, 0), ("m2", 2, 0), ("k1", 3, 1),
+    ("bg", 1), ("k2", 2, 0), ("k3", 1, 0), ("k2", 3, 0), ("m2", 1, 1), ("k2", 3, 1), ("bg", 0),
+    ("m2", 2, 2), ("k3", 2, 0), ("k3", 3, 0), ("m2", 1, 2), ("k3", 3, 1), ("k4", 0), ("m2", 2, 1),
+    ("m2_out", 2), ("m2", 0, 1), ("m2", 0, 2), ("m2", 1, 0), ("m2_out", 1), ("m2", 0, 0), ("m2_out", 0),
+    ("k4", 1),
 )
 
 

time: 110 us -> 111 us (level); the launches traced: 110 us -> 110 us
  no operation moved by 1% of the time
where the time goes in v3:
time: 111 us; the launch traced here: 110 us
  Pallas kernels  109 us (98%)
    pallas_call x1, Pallas kernels, local(): pl.pallas_call(kernel, out_shape=shapes, in_specs=[hbm, hbm, vmem, hbm],...  104 us
    pallas_call x1, Pallas kernels, local(): pl.pallas_call(hand_out, out_shape=shapes, in_specs=[hbm] * 4, out_specs=...  4.93 us

profile of v3, /device:TPU:8, one launch (start us, length us, event | category | flops | bytes accessed | tf_op | source)
XLA Modules:
  0.0 109.7 jit_solution(8922391401984571569)
XLA Ops:
  0.6 103.9 %ffn.1 = (bf16[4,2,16,1536]{3,2,1,0:T(8,128)(2,1)}, bf16[2,16,1536]{2,1,0:T(8,128)(2,1)}, bf16[1536,1536]{1,0:T(8,128)(2,1)}, f32[12,128]{1,0:T(8,128)}) custom-call(bf16[2,16,1536]{2,1,0:T(8,128)(2,1)} %bitcast.7, bf16[1536,1536]{1,0:T(8,128)(2,1)} %w_hbm.1, f32[12,128]{1,0:T(8,128)} %bitcast.8, bf16[4,2,16,1536]{3,2,1,0:T(8,128)(2,1)} %bitcast.6), custom_call_target="tpu_custom_call" | custom-call | tf_op jit(solution)/shard_map/ffn/pallas_call | solution.py:449
  104.6 4.9 %hand_out.1 = (bf16[4,2,16,1536]{3,2,1,0:T(8,128)(2,1)}, bf16[2,16,1536]{2,1,0:T(8,128)(2,1)}, bf16[1536,1536]{1,0:T(8,128)(2,1)}, f32[12,128]{1,0:T(8,128)}) custom-call(bf16[4,2,16,1536]{3,2,1,0:T(8,128)(2,1)} %get-tuple-element.12.refs_0_, bf16[2,16,1536]{2,1,0:T(8,128)(2,1)} %get-tuple-element.13.refs_1_, bf16[1536,1536]{1,0:T(8,128)(2,1)} %get-tuple-element.14.refs_2_, ...), custom_call_target="tpu_custom_call" | custom-call | tf_op jit(solution)/shard_map/hand_out/pallas_call | solution.py:465
